TPU v7x, 32 devices: a whole 2x2x4 slice. The times are simulated.
32 devices in a mesh: groups: 2 (over y), seq: 4 (over z), tensor: 4 (over x, core).
Axes of the slice: x: 2, y: 2, z: 4, core: 2. Of those that a mesh axis runs over, the one named last changes fastest.
Arguments:
- residual_in: float32 [1024, 4096], P(('groups', 'seq'), 'tensor'), parts along dimension 0, may hold values from -48 to 48
- norm_gain: float32 [4096], replicated, may hold values from 0.1 to 1.9
- in_weight: bfloat16 [3, 4096, 2048], P(None, 'seq', 'tensor'), may hold values from -0.09375 to 0.09375
- short_taps: float32 [3, 3, 2048], P(None, None, 'tensor'), may hold values from -3 to 3
- long_filter: float32 [2048, 512], P(('tensor', 'seq')), may hold values from -0.25 to 0.25
- out_weight: bfloat16 [4096, 2048], P('seq', 'tensor'), may hold values from -0.125 to 0.125
Outputs:
- block_out: float32 [1024, 4096], P(('groups', 'seq'), 'tensor'), parts along dimension 0
There are 2 independent parts, one for each index of `groups`. A program takes and returns all parts, laid end to end along the dimension named above; an argument that names none is the same for every part. Nothing has to cross between parts.
All inputs are finite; a program needn't handle non-finite values.
Results may differ from a plain program's by a relative error of at most 0.015.
Values may be sent and summed in bfloat16 or wider, within the bound.
A program may use at most 64 MiB of HBM per device.

v0:
```python
import math

import jax
import jax.numpy as jnp
import ml_dtypes
import numpy as np
from jax import lax
from jax.experimental import pallas as pl
from jax.experimental.pallas import tpu as pltpu
from jax.sharding import PartitionSpec as P

EPSILON = 1e-05


def shifted(value, axis, by):
    length = lax.axis_size(axis)
    pairs = [(i, i + by) for i in range(length) if 0 <= i + by < length]
    return lax.ppermute(value, axis, pairs)


def exact_product(form, left, right):
    return jnp.einsum(form, left, right, precision=lax.Precision.HIGHEST)


def angle_tables(modulus, count_a, count_b):
    index_a = jnp.arange(count_a, dtype=jnp.int32)[:, None]
    index_b = jnp.arange(count_b, dtype=jnp.int32)[None, :]
    theta = (index_a * index_b % modulus).astype(jnp.float32) * (2.0 * math.pi / modulus)
    return (jnp.cos(theta), jnp.sin(theta))


def split_length(full_length):
    low_factor = 1
    while full_length % (4 * low_factor) == 0 and 4 * low_factor * low_factor <= full_length:
        low_factor = low_factor * 2
    return (low_factor, full_length // low_factor)


def forward_spectrum(signal, low_factor, high_factor, all_tables):
    cos_high, sin_high, cos_twist, sin_twist, cos_low, sin_low = all_tables
    channel_count = signal.shape[0]
    blocks = signal.reshape(channel_count, high_factor // 2, low_factor)
    real_a = exact_product("cmp,mk->cpk", blocks, cos_high)
    imag_a = -exact_product("cmp,mk->cpk", blocks, sin_high)
    real_b = real_a * cos_twist + imag_a * sin_twist
    imag_b = imag_a * cos_twist - real_a * sin_twist
    real_x = exact_product("cpk,pj->cjk", real_b, cos_low) + exact_product(
        "cpk,pj->cjk", imag_b, sin_low
    )
    imag_x = exact_product("cpk,pj->cjk", imag_b, cos_low) - exact_product(
        "cpk,pj->cjk", real_b, sin_low
    )
    return (real_x, imag_x)


def inverse_signal(real_x, imag_x, low_factor, high_factor, all_tables):
    cos_high, sin_high, cos_twist, sin_twist, cos_low, sin_low = all_tables
    channel_count = real_x.shape[0]
    real_b = exact_product("cjk,pj->cpk", real_x, cos_low) - exact_product(
        "cjk,pj->cpk", imag_x, sin_low
    )
    imag_b = exact_product("cjk,pj->cpk", real_x, sin_low) + exact_product(
        "cjk,pj->cpk", imag_x, cos_low
    )
    real_c = real_b * cos_twist - imag_b * sin_twist
    imag_c = real_b * sin_twist + imag_b * cos_twist
    result = exact_product("cpk,mk->cmp", real_c, cos_high) - exact_product(
        "cpk,mk->cmp", imag_c, sin_high
    )
    full_length = low_factor * high_factor
    return (result / full_length).reshape(channel_count, full_length // 2)


def shards(residual_in, norm_gain, in_weight, short_taps, long_filter, out_weight):
    row_count, local_width = residual_in.shape
    full_rows = lax.all_gather(
        residual_in.astype(jnp.bfloat16), "tensor", axis=1, tiled=True
    ).astype(residual_in.dtype)
    mean_sq = jnp.mean(full_rows * full_rows, axis=1, keepdims=True)
    normed = (full_rows * lax.rsqrt(mean_sq + EPSILON) * norm_gain).astype(jnp.bfloat16)
    projected = jnp.einsum(
        "rd,sdc->scr",
        normed,
        lax.all_gather(in_weight, "seq", axis=1, tiled=True),
        preferred_element_type=jnp.float32,
    )
    reach = short_taps.shape[1] - 1
    earlier = shifted(projected[:, :, row_count - reach :], "seq", 1)
    extended = jnp.concatenate([earlier, projected], axis=2)
    mixed = short_taps[:, 0, :, None] * projected
    for offset in range(1, reach + 1):
        mixed = (
            mixed
            + short_taps[:, offset, :, None]
            * extended[:, :, reach - offset : reach - offset + row_count]
        )
    query = mixed[0]
    product_kv = mixed[1] * mixed[2]
    by_channel = lax.all_to_all(
        product_kv.astype(jnp.bfloat16), "seq", split_axis=0, concat_axis=1, tiled=True
    ).astype(product_kv.dtype)
    full_length = 2 * by_channel.shape[1]
    low_factor, high_factor = split_length(full_length)
    cos_high, sin_high = angle_tables(high_factor, high_factor // 2, high_factor)
    cos_twist, sin_twist = angle_tables(full_length, low_factor, high_factor)
    cos_low, sin_low = angle_tables(low_factor, low_factor, low_factor)
    all_tables = (cos_high, sin_high, cos_twist, sin_twist, cos_low, sin_low)
    signal_real, signal_imag = forward_spectrum(by_channel, low_factor, high_factor, all_tables)
    filter_real, filter_imag = forward_spectrum(long_filter, low_factor, high_factor, all_tables)
    conv = inverse_signal(
        signal_real * filter_real - signal_imag * filter_imag,
        signal_real * filter_imag + signal_imag * filter_real,
        low_factor,
        high_factor,
        all_tables,
    )
    returned = lax.all_to_all(
        conv.astype(jnp.bfloat16), "seq", split_axis=1, concat_axis=0, tiled=True
    ).astype(conv.dtype)
    gated = (query * returned).astype(jnp.bfloat16)
    terms = jnp.einsum(
        "cr,nc->rn",
        gated,
        lax.all_gather(out_weight, "seq", axis=0, tiled=True),
        preferred_element_type=jnp.float32,
    )
    summed = lax.psum_scatter(
        terms.astype(jnp.bfloat16), "tensor", scatter_dimension=1, tiled=True
    ).astype(jnp.float32)
    return residual_in + summed


MESH = pl.DeviceIdType.MESH


def transform_tables(length):
    index = np.arange(length)
    turns = ((2 * index[:, None] + 1) * index[None, :]) % (4 * length)
    theta = turns.astype(np.float64) * (math.pi / (2 * length))
    table = np.concatenate([np.cos(theta), np.sin(theta)], axis=0).astype(np.float32)
    high = table.astype(ml_dtypes.bfloat16)
    low = (table - high.astype(np.float32)).astype(ml_dtypes.bfloat16)
    return (high, low, np.ascontiguousarray(high.T), np.ascontiguousarray(low.T))


def two_parts(value):
    high = value.astype(jnp.bfloat16)
    low = (value - high.astype(jnp.float32)).astype(jnp.bfloat16)
    return (high, low)


def matmul(left, right):
    return jnp.dot(left, right, preferred_element_type=jnp.float32)


def matmul_nt(left, right):
    return lax.dot_general(left, right, (((1,), (1,)), ((), ())), preferred_element_type=jnp.float32)


def block_kernel(
    x_hbm, gain_hbm, w_hbm, taps_hbm, filter_hbm, wo_hbm, ah_hbm, al_hbm, bh_hbm, bl_hbm,
    out_ref,
    x_ref, gain_ref, taps_ref, filter_ref, wv, wo, ah, al, bh, bl, xb, xg, part, sendb, inbox, squares, spectrum,
    gathered, terms, terms_acc, sibling_in, cross_in, final_in,
    load_sem, x_send, x_recv, p_send, p_recv, q_send, q_recv,
    g_right, g_left, g_recv, t_send, t_recv,
):
    s = lax.axis_index("seq")
    t = lax.axis_index("tensor")
    n = 4
    rows, width = x_ref.shape
    ch = filter_ref.shape[0]
    length = filter_ref.shape[1]
    sib = t + 1 - 2 * lax.rem(t, 2)
    far = lax.rem(t + 2, n)
    far_sib = lax.rem(sib + 2, n)

    chunks = 4
    step = rows // chunks

    def lanes(i):
        return pl.ds(pl.multiple_of(i * ch, 128), ch)

    loads = []
    for d in range(n):
        for j in range(3):
            loads.append(pltpu.make_async_copy(
                w_hbm.at[(j + 1) % 3, :, pl.ds(d * ch, ch)],
                wv.at[d, :, pl.ds(j * ch, ch)],
                load_sem.at[d * 3 + j],
            ))
    for i, (source, target) in enumerate((
        (ah_hbm, ah), (al_hbm, al), (wo_hbm, wo), (bh_hbm, bh), (bl_hbm, bl),
        (x_hbm, x_ref), (filter_hbm, filter_ref), (taps_hbm.at[:, :, lanes(s)], taps_ref),
        (gain_hbm.at[:, pl.ds(pl.multiple_of(s * width, 128), width)], gain_ref),
    )):
        loads.append(pltpu.make_async_copy(source, target, load_sem.at[3 * n + i]))
    x_load, filter_load, taps_load, gain_load = loads[3 * n + 5:]
    x_load.start()

    barrier = pltpu.get_barrier_semaphore()
    for k in range(1, n):
        pl.semaphore_signal(barrier, inc=1, device_id={"seq": lax.rem(s + k, n), "tensor": t}, device_id_type=MESH)
        pl.semaphore_signal(barrier, inc=1, device_id={"seq": s, "tensor": lax.rem(t + k, n)}, device_id_type=MESH)

    @pl.when(s != t)
    def _():
        pl.semaphore_signal(barrier, inc=1, device_id={"seq": t, "tensor": s}, device_id_type=MESH)

    x_load.wait()
    xb[...] = x_ref[...].astype(jnp.bfloat16)

    @pl.when(s != t)
    def _():
        pl.semaphore_wait(barrier, 2 * n - 1)

    @pl.when(s == t)
    def _():
        pl.semaphore_wait(barrier, 2 * n - 2)

    def remote(source, target, send, recv, to_s, to_t):
        return pltpu.make_async_remote_copy(
            src_ref=source, dst_ref=target, send_sem=send, recv_sem=recv,
            device_id={"seq": to_s, "tensor": to_t}, device_id_type=MESH,
        )

    def piece(h):
        return pl.ds(h * step, step)

    def swap(h, slot):
        return remote(
            xb.at[piece(h)], xg.at[slot, piece(h)], x_send.at[0, h], x_recv.at[slot, h], t, s
        )

    @pl.when(s != t)
    def _():
        for h in range(chunks):
            swap(h, s).start()

    gain_load.start()
    for load in loads[:3 * n] + [filter_load] + loads[3 * n:3 * n + 2] + [taps_load] + loads[3 * n + 2:3 * n + 5]:
        load.start()

    def slot_copy(slot, which, to_t, h):
        return remote(
            xg.at[slot, piece(h)], xg.at[slot, piece(h)], x_send.at[which, h], x_recv.at[slot, h], s, to_t
        )

    @pl.when(s == t)
    def _():
        xg[t] = xb[...]

    for h in range(chunks):
        @pl.when(s != t)
        def _():
            swap(h, t).wait_recv()

        slot_copy(t, 1, far, h).start()
        slot_copy(t, 2, sib, h).start()

    for load in loads[: 3 * n]:
        load.wait()
    gain_load.wait()
    gain = gain_ref[...]
    ones = jnp.ones((8, width), jnp.bfloat16)

    def p_copy(p, d, slot):
        return remote(sendb.at[p, d], inbox.at[p, slot], p_send.at[p, d], p_recv.at[p, slot], d, t)

    others = [lax.rem(s + k, n) for k in (2, 1, 3)]

    def dots(p):
        features = xg[p].astype(jnp.float32)
        sh, sl = two_parts(features * features)
        squares[s, :, pl.ds(pl.multiple_of(p * rows, 128), rows)] = matmul_nt(ones, sh) + matmul_nt(ones, sl)
        y = (features * gain).astype(jnp.bfloat16)

        @pl.loop(0, n)
        def _(d):
            part[p, d] = matmul(y, wv[d])

        for d in others:
            sendb[p, d] = part[p, d].astype(jnp.bfloat16)
            p_copy(p, d, s).start()

    def total(p):
        for k in others:
            p_copy(p, k, k).wait_recv()
        value = part[p, s]
        for k in others:
            value = value + inbox[p, k].astype(jnp.float32)
        part[p, s] = value

    order = (t, sib, far, far_sib)
    dots(t)
    for h in range(chunks):
        slot_copy(far, 1, far, h).wait_recv()
        slot_copy(far, 3, sib, h).start()
    for h in range(chunks):
        slot_copy(sib, 2, sib, h).wait_recv()
    dots(sib)
    dots(far)
    for h in range(chunks):
        slot_copy(far_sib, 3, sib, h).wait_recv()
    dots(far_sib)

    q_copies = []
    for k in range(1, n):
        q_copy = remote(squares.at[s], squares.at[s], q_send.at[k], q_recv.at[s], lax.rem(s + k, n), t)
        q_copy.start()
        q_copies.append(q_copy)
    filter_load.wait()
    fh, fl = two_parts(filter_ref[...])
    loads[3 * n].wait()
    loads[3 * n + 1].wait()
    spectrum[...] = matmul_nt(ah[...], fh) + matmul_nt(ah[...], fl) + matmul_nt(al[...], fh)


    for k in range(1, n):
        other = lax.rem(s + k, n)
        remote(squares.at[other], squares.at[other], q_send.at[k], q_recv.at[other], other, t).wait_recv()
    all_squares = squares[0] + squares[1] + squares[2] + squares[3]
    scale = lax.rsqrt(all_squares * (1.0 / (n * width)) + EPSILON)
    scale = jnp.transpose(jnp.broadcast_to(scale[0:1], (ch, length)))
    taps_load.wait()
    for p in order:
        total(p)

    row = lax.broadcasted_iota(jnp.int32, (length, ch), 0)

    def filtered(j):
        at = (j + 2) % 3 * ch
        projected = jnp.concatenate([part[p, s, :, at:at + ch] for p in range(n)], axis=0) * scale
        taps = [taps_ref[j, o:o + 1, :] for o in range(3)]
        value = taps[0] * projected
        for o in range(1, 3):
            value = value + taps[o] * jnp.where(row >= o, pltpu.roll(projected, o, 0), 0.0)
        return value

    kh, kl = two_parts(filtered(1) * filtered(2))
    both = matmul(ah[...], jnp.concatenate([kh, kl], axis=1))
    signal = both[:, :ch] + both[:, ch:] + matmul(al[...], kh)
    a, b = signal[:length], signal[length:]
    c, e = spectrum[:length], spectrum[length:]
    yh, yl = two_parts(jnp.concatenate([a * c - b * e, a * e + b * c], axis=0))
    for load in loads[3 * n + 2:3 * n + 5]:
        load.wait()
    both = matmul(bh[...], jnp.concatenate([yh, yl], axis=1))
    conv = (both[:, :ch] + both[:, ch:] + matmul(bl[...], yh)) * (1.0 / length)
    query = filtered(0)

    gathered[s] = (query * conv).astype(jnp.bfloat16)

    def g_copy(i, up):
        sems = g_right if up else g_left
        return remote(
            gathered.at[i], gathered.at[i], sems.at[i], g_recv.at[i],
            s + 1 if up else s - 1, t,
        )

    @pl.when(s < n - 1)
    def _():
        g_copy(s, True).start()

    @pl.when(s > 0)
    def _():
        g_copy(s, False).start()

    for k in range(1, n):
        @pl.when(s - k >= 0)
        def _():
            g_copy(s - k, True).wait_recv()

            @pl.when(s < n - 1)
            def _():
                g_copy(s - k, True).start()

        @pl.when(s + k < n)
        def _():
            g_copy(s + k, False).wait_recv()

            @pl.when(s > 0)
            def _():
                g_copy(s + k, False).start()

    def term(p):
        at = pl.ds(pl.multiple_of(p * rows, 128), rows)
        return matmul_nt(jnp.concatenate([gathered[i, at] for i in range(n)], axis=1), wo[...])

    def hop(which, target, to_s, to_t, h):
        return remote(
            terms.at[which, piece(h)], target.at[piece(h)], t_send.at[which, h], t_recv.at[which, h], to_s, to_t
        )

    def far_out(h):
        return hop(0, sibling_in.at[0], s, sib, h)

    def own_out(h):
        return hop(1, sibling_in.at[1], s, sib, h)

    def cross(h):
        return hop(2, cross_in, s, far, h)

    def final(h):
        return hop(3, final_in, t, s, h)

    terms[0] = term(far_sib).astype(jnp.bfloat16)
    for h in range(chunks):
        far_out(h).start()
    terms_acc[...] = term(far)
    for h in range(chunks):
        far_out(h).wait_recv()
        terms[2, piece(h)] = (
            terms_acc[piece(h)] + sibling_in[0, piece(h)].astype(jnp.float32)
        ).astype(jnp.bfloat16)
        cross(h).start()
    terms[1] = term(sib).astype(jnp.bfloat16)
    for h in range(chunks):
        own_out(h).start()
    terms_acc[...] = term(t)
    for h in range(chunks):
        own_out(h).wait_recv()
        terms_acc[piece(h)] += sibling_in[1, piece(h)].astype(jnp.float32)
    for h in range(chunks):
        cross(h).wait_recv()
        value = terms_acc[piece(h)] + cross_in[piece(h)].astype(jnp.float32)

        @pl.when(s != t)
        def _():
            terms[3, piece(h)] = value.astype(jnp.bfloat16)
            final(h).start()

        @pl.when(s == t)
        def _():
            out_ref[piece(h)] = x_ref[piece(h)] + value

    @pl.when(s != t)
    def _():
        for h in range(chunks):
            final(h).wait_recv()
            out_ref[piece(h)] = x_ref[piece(h)] + final_in[piece(h)].astype(jnp.float32)
        for h in range(chunks):
            swap(h, s).wait_send()
            final(h).wait_send()

    for h in range(chunks):
        for copy in (
            slot_copy(t, 1, far, h), slot_copy(t, 2, sib, h), slot_copy(far, 3, sib, h),
            far_out(h), own_out(h), cross(h),
        ):
            copy.wait_send()
    for copy in q_copies:
        copy.wait_send()
    for p in order:
        for d in others:
            p_copy(p, d, s).wait_send()

    @pl.loop(0, n)
    def _(i):
        @pl.when((i <= s) & (s < n - 1))
        def _():
            g_copy(i, True).wait_send()

        @pl.when((i >= s) & (s > 0))
        def _():
            g_copy(i, False).wait_send()


def kernel_shards(residual_in, norm_gain, in_weight, short_taps, long_filter, out_weight):
    n = 4
    rows, width = residual_in.shape
    ch, length = long_filter.shape
    tables = [jnp.asarray(table) for table in transform_tables(length)]
    vmem, hbm = pl.BlockSpec(memory_space=pltpu.VMEM), pl.BlockSpec(memory_space=pl.ANY)
    dma = pltpu.SemaphoreType.DMA
    bf16, f32 = jnp.bfloat16, jnp.float32
    return pl.pallas_call(
        block_kernel,
        out_shape=jax.ShapeDtypeStruct((rows, width), f32),
        in_specs=[hbm] * 10,
        out_specs=vmem,
        scratch_shapes=[
            pltpu.VMEM((rows, width), f32),
            pltpu.VMEM((1, width), f32),
            pltpu.VMEM(short_taps.shape[:2] + (ch,), f32),
            pltpu.VMEM((ch, length), f32),
            pltpu.VMEM((n, width, 3 * ch), bf16),
            pltpu.VMEM(out_weight.shape, bf16),
            pltpu.VMEM((2 * length, length), bf16),
            pltpu.VMEM((2 * length, length), bf16),
            pltpu.VMEM((length, 2 * length), bf16),
            pltpu.VMEM((length, 2 * length), bf16),
            pltpu.VMEM((rows, width), bf16),
            pltpu.VMEM((n, rows, width), bf16),
            pltpu.VMEM((n, n, rows, 3 * ch), f32),
            pltpu.VMEM((n, n, rows, 3 * ch), bf16),
            pltpu.VMEM((n, n, rows, 3 * ch), bf16),
            pltpu.VMEM((n, 8, length), f32),
            pltpu.VMEM((2 * length, ch), f32),
            pltpu.VMEM((n, length, ch), bf16),
            pltpu.VMEM((n, rows, width), bf16),
            pltpu.VMEM((rows, width), f32),
            pltpu.VMEM((2, rows, width), bf16),
            pltpu.VMEM((rows, width), bf16),
            pltpu.VMEM((rows, width), bf16),
            dma((3 * n + 9,)), dma((n, n)), dma((n, n)), dma((n, n)), dma((n, n)),
            dma((n,)), dma((n,)), dma((n,)), dma((n,)), dma((n,)), dma((n, n)), dma((n, n)),
        ],
        compiler_params=pltpu.CompilerParams(
            collective_id=0, has_side_effects=True, vmem_limit_bytes=60 * 1024 * 1024
        ),
    )(residual_in, norm_gain[None], in_weight, short_taps, long_filter, out_weight, *tables)


def solution(mesh):
    square = mesh.shape["seq"] == 4 and mesh.shape["tensor"] == 4
    return jax.shard_map(
        kernel_shards if square else shards,
        mesh=mesh,
        in_specs=(
            P(("groups", "seq"), "tensor"),
            P(),
            P(None, "seq", "tensor"),
            P(None, None, "tensor"),
            P(("tensor", "seq"), None),
            P("seq", "tensor"),
        ),
        out_specs=P(("groups", "seq"), "tensor"),
        check_vma=False,
    )
```

profile of v0, /device:TPU:16, one launch (start us, length us, event | category | flops | bytes accessed | tf_op | source)
XLA Modules:
  0.0 87.5 jit_solution(13421883552013105802)
XLA Ops:
  0.0 85.6 %shard_map.100 = f32[128,1024]{1,0:T(8,128)} custom-call(f32[128,1024]{1,0:T(8,128)} %x_hbm.1, f32[1,4096]{1,0:T(1,128)} %bitcast.1, bf16[3,1024,512]{2,1,0:T(8,128)(2,1)} %w_hbm.1, f32[3,3,512]{2,1,0:T(4,128)} %taps_hbm.1, f32[128,512]{1,0:T(8,128)} %filter_hbm.1, bf16[1024,512]{1,0:T(8,128)(2,1)} %wo_hbm.1, bf16[1024,512]{1,0:T(8,128)(2,1)} %constant.8.clone.ah_hbm, ...), custom_call_target="tpu_custom_call" | custom-call | tf_op jit(solution)/shard_map/pallas_call | solution.py:477
  85.7 1.9 %copy.12 = f32[128,1024]{1,0:T(8,128)} copy(f32[128,1024]{1,0:T(8,128)} %shard_map.100) | data formatting | bytes 1048576
where the time goes:
time: 87.7 us; the launch traced here: 87.5 us
  Pallas kernels  85.6 us (98%)
  local copies, waits for them, and re-layouts  1.89 us (2%)
    pallas_call x1, Pallas kernels, kernel_shards(): pl.pallas_call(block_kernel, out_shape=jax.ShapeDtypeStruct((rows, width)...  85.6 us
    unnamed x1, local copies, waits for them, and re-layouts  1.89 us

commit v1 on v0

--- a/solution.py
+++ b/solution.py
@@ -160,10 +160,10 @@
 def block_kernel(
     x_hbm, gain_hbm, w_hbm, taps_hbm, filter_hbm, wo_hbm, ah_hbm, al_hbm, bh_hbm, bl_hbm,
     out_ref,
-    x_ref, gain_ref, taps_ref, filter_ref, wv, wo, ah, al, bh, bl, xb, xg, part, sendb, inbox, squares, spectrum,
+    x_ref, gain_ref, taps_ref, filter_ref, wv, wo, ah, al, bh, bl, xb, xg, part, sendb, inbox, squares, spectrum, query,
     gathered, terms, terms_acc, sibling_in, cross_in, final_in,
     load_sem, x_send, x_recv, p_send, p_recv, q_send, q_recv,
-    g_right, g_left, g_recv, t_send, t_recv,
+    g_send, g_recv, t_send, t_recv,
 ):
     s = lax.axis_index("seq")
     t = lax.axis_index("tensor")
@@ -345,46 +345,30 @@
     yh, yl = two_parts(jnp.concatenate([a * c - b * e, a * e + b * c], axis=0))
     for load in loads[3 * n + 2:3 * n + 5]:
         load.wait()
-    both = matmul(bh[...], jnp.concatenate([yh, yl], axis=1))
-    conv = (both[:, :ch] + both[:, ch:] + matmul(bl[...], yh)) * (1.0 / length)
-    query = filtered(0)
-
-    gathered[s] = (query * conv).astype(jnp.bfloat16)
-
-    def g_copy(i, up):
-        sems = g_right if up else g_left
+    query[...] = filtered(0)
+    y_parts = jnp.concatenate([yh, yl], axis=1)
+    send_order = (far_sib, far, sib, t)
+
+    def block_rows(p):
+        return pl.ds(pl.multiple_of(p * rows, 128), rows)
+
+    def g_copy(p, to, slot):
         return remote(
-            gathered.at[i], gathered.at[i], sems.at[i], g_recv.at[i],
-            s + 1 if up else s - 1, t,
+            gathered.at[slot, block_rows(p)], gathered.at[slot, block_rows(p)],
+            g_send.at[p, to], g_recv.at[p, slot], to, t,
         )
 
-    @pl.when(s < n - 1)
-    def _():
-        g_copy(s, True).start()
-
-    @pl.when(s > 0)
-    def _():
-        g_copy(s, False).start()
-
-    for k in range(1, n):
-        @pl.when(s - k >= 0)
-        def _():
-            g_copy(s - k, True).wait_recv()
-
-            @pl.when(s < n - 1)
-            def _():
-                g_copy(s - k, True).start()
-
-        @pl.when(s + k < n)
-        def _():
-            g_copy(s + k, False).wait_recv()
-
-            @pl.when(s > 0)
-            def _():
-                g_copy(s + k, False).start()
+    for p in send_order:
+        both = matmul(bh[block_rows(p)], y_parts)
+        conv = (both[:, :ch] + both[:, ch:] + matmul(bl[block_rows(p)], yh)) * (1.0 / length)
+        gathered[s, block_rows(p)] = (query[block_rows(p)] * conv).astype(jnp.bfloat16)
+        for to in others:
+            g_copy(p, to, s).start()
 
     def term(p):
-        at = pl.ds(pl.multiple_of(p * rows, 128), rows)
+        at = block_rows(p)
+        for k in others:
+            g_copy(p, k, k).wait_recv()
         return matmul_nt(jnp.concatenate([gathered[i, at] for i in range(n)], axis=1), wo[...])
 
     def hop(which, target, to_s, to_t, h):
@@ -455,15 +439,9 @@
         for d in others:
             p_copy(p, d, s).wait_send()
 
-    @pl.loop(0, n)
-    def _(i):
-        @pl.when((i <= s) & (s < n - 1))
-        def _():
-            g_copy(i, True).wait_send()
-
-        @pl.when((i >= s) & (s > 0))
-        def _():
-            g_copy(i, False).wait_send()
+    for p in order:
+        for to in others:
+            g_copy(p, to, s).wait_send()
 
 
 def kernel_shards(residual_in, norm_gain, in_weight, short_taps, long_filter, out_weight):
@@ -497,6 +475,7 @@
             pltpu.VMEM((n, n, rows, 3 * ch), bf16),
             pltpu.VMEM((n, 8, length), f32),
             pltpu.VMEM((2 * length, ch), f32),
+            pltpu.VMEM((length, ch), f32),
             pltpu.VMEM((n, length, ch), bf16),
             pltpu.VMEM((n, rows, width), bf16),
             pltpu.VMEM((rows, width), f32),
@@ -504,7 +483,7 @@
             pltpu.VMEM((rows, width), bf16),
             pltpu.VMEM((rows, width), bf16),
             dma((3 * n + 9,)), dma((n, n)), dma((n, n)), dma((n, n)), dma((n, n)),
-            dma((n,)), dma((n,)), dma((n,)), dma((n,)), dma((n,)), dma((n, n)), dma((n, n)),
+            dma((n,)), dma((n,)), dma((n, n)), dma((n, n)), dma((n, n)), dma((n, n)),
         ],
         compiler_params=pltpu.CompilerParams(
             collective_id=0, has_side_effects=True, vmem_limit_bytes=60 * 1024 * 1024

time: 87.7 us -> 89.4 us (1.019)
  the two profiles are of different devices: /device:TPU:16 before, /device:TPU:2 now
where the time goes in v1:
time: 89.4 us; the launch traced here: 89.2 us
  Pallas kernels  87.3 us (98%)
  local copies, waits for them, and re-layouts  1.89 us (2%)
    pallas_call x1, Pallas kernels, kernel_shards(): pl.pallas_call(block_kernel, out_shape=jax.ShapeDtypeStruct((rows, width)...  87.3 us
    unnamed x1, local copies, waits for them, and re-layouts  1.89 us

profile of v1, /device:TPU:2, one launch (start us, length us, event | category | flops | bytes accessed | tf_op | source)
XLA Modules:
  0.0 89.2 jit_solution(4758777447461167126)
XLA Ops:
  0.0 87.3 %shard_map.100 = f32[128,1024]{1,0:T(8,128)} custom-call(f32[128,1024]{1,0:T(8,128)} %x_hbm.1, f32[1,4096]{1,0:T(1,128)} %bitcast.1, bf16[3,1024,512]{2,1,0:T(8,128)(2,1)} %w_hbm.1, f32[3,3,512]{2,1,0:T(4,128)} %taps_hbm.1, f32[128,512]{1,0:T(8,128)} %filter_hbm.1, bf16[1024,512]{1,0:T(8,128)(2,1)} %wo_hbm.1, bf16[1024,512]{1,0:T(8,128)(2,1)} %constant.8.clone.ah_hbm, ...), custom_call_target="tpu_custom_call" | custom-call | tf_op jit(solution)/shard_map/pallas_call | solution.py:455
  87.3 1.9 %copy.12 = f32[128,1024]{1,0:T(8,128)} copy(f32[128,1024]{1,0:T(8,128)} %shard_map.100) | data formatting | bytes 1048576

commit v2 on v0

--- a/solution.py
+++ b/solution.py
@@ -160,7 +160,7 @@
 def block_kernel(
     x_hbm, gain_hbm, w_hbm, taps_hbm, filter_hbm, wo_hbm, ah_hbm, al_hbm, bh_hbm, bl_hbm,
     out_ref,
-    x_ref, gain_ref, taps_ref, filter_ref, wv, wo, ah, al, bh, bl, xb, xg, part, sendb, inbox, squares, spectrum,
+    x_ref, gain_ref, taps_ref, filter_ref, wv, wo, ah, al, bh, bl, xb, xg, part, send_kv, send_q, inbox_kv, inbox_q, squares, spectrum,
     gathered, terms, terms_acc, sibling_in, cross_in, final_in,
     load_sem, x_send, x_recv, p_send, p_recv, q_send, q_recv,
     g_right, g_left, g_recv, t_send, t_recv,
@@ -264,8 +264,13 @@
     gain = gain_ref[...]
     ones = jnp.ones((8, width), jnp.bfloat16)
 
-    def p_copy(p, d, slot):
-        return remote(sendb.at[p, d], inbox.at[p, slot], p_send.at[p, d], p_recv.at[p, slot], d, t)
+    cuts = (slice(0, 2 * ch), slice(2 * ch, 3 * ch))
+    sendb, inbox = (send_kv, send_q), (inbox_kv, inbox_q)
+
+    def p_copy(p, d, slot, q):
+        return remote(
+            sendb[q].at[p, d], inbox[q].at[p, slot], p_send.at[q, p, d], p_recv.at[q, p, slot], d, t
+        )
 
     others = [lax.rem(s + k, n) for k in (2, 1, 3)]
 
@@ -280,16 +285,17 @@
             part[p, d] = matmul(y, wv[d])
 
         for d in others:
-            sendb[p, d] = part[p, d].astype(jnp.bfloat16)
-            p_copy(p, d, s).start()
-
-    def total(p):
+            sendb[0][p, d] = part[p, d, :, cuts[0]].astype(jnp.bfloat16)
+            p_copy(p, d, s, 0).start()
+            sendb[1][p, d] = part[p, d, :, cuts[1]].astype(jnp.bfloat16)
+
+    def total(p, q):
         for k in others:
-            p_copy(p, k, k).wait_recv()
-        value = part[p, s]
+            p_copy(p, k, k, q).wait_recv()
+        value = part[p, s, :, cuts[q]]
         for k in others:
-            value = value + inbox[p, k].astype(jnp.float32)
-        part[p, s] = value
+            value = value + inbox[q][p, k].astype(jnp.float32)
+        part[p, s, :, cuts[q]] = value
 
     order = (t, sib, far, far_sib)
     dots(t)
@@ -324,7 +330,13 @@
     scale = jnp.transpose(jnp.broadcast_to(scale[0:1], (ch, length)))
     taps_load.wait()
     for p in order:
-        total(p)
+        for d in others:
+            p_copy(p, d, s, 0).wait_send()
+    for p in order:
+        for d in others:
+            p_copy(p, d, s, 1).start()
+    for p in order:
+        total(p, 0)
 
     row = lax.broadcasted_iota(jnp.int32, (length, ch), 0)
 
@@ -347,6 +359,8 @@
         load.wait()
     both = matmul(bh[...], jnp.concatenate([yh, yl], axis=1))
     conv = (both[:, :ch] + both[:, ch:] + matmul(bl[...], yh)) * (1.0 / length)
+    for p in order:
+        total(p, 1)
     query = filtered(0)
 
     gathered[s] = (query * conv).astype(jnp.bfloat16)
@@ -453,7 +467,7 @@
         copy.wait_send()
     for p in order:
         for d in others:
-            p_copy(p, d, s).wait_send()
+            p_copy(p, d, s, 1).wait_send()
 
     @pl.loop(0, n)
     def _(i):
@@ -493,8 +507,10 @@
             pltpu.VMEM((rows, width), bf16),
             pltpu.VMEM((n, rows, width), bf16),
             pltpu.VMEM((n, n, rows, 3 * ch), f32),
-            pltpu.VMEM((n, n, rows, 3 * ch), bf16),
-            pltpu.VMEM((n, n, rows, 3 * ch), bf16),
+            pltpu.VMEM((n, n, rows, 2 * ch), bf16),
+            pltpu.VMEM((n, n, rows, ch), bf16),
+            pltpu.VMEM((n, n, rows, 2 * ch), bf16),
+            pltpu.VMEM((n, n, rows, ch), bf16),
             pltpu.VMEM((n, 8, length), f32),
             pltpu.VMEM((2 * length, ch), f32),
             pltpu.VMEM((n, length, ch), bf16),
@@ -503,7 +519,7 @@
             pltpu.VMEM((2, rows, width), bf16),
             pltpu.VMEM((rows, width), bf16),
             pltpu.VMEM((rows, width), bf16),
-            dma((3 * n + 9,)), dma((n, n)), dma((n, n)), dma((n, n)), dma((n, n)),
+            dma((3 * n + 9,)), dma((n, n)), dma((n, n)), dma((2, n, n)), dma((2, n, n)),
             dma((n,)), dma((n,)), dma((n,)), dma((n,)), dma((n,)), dma((n, n)), dma((n, n)),
         ],
         compiler_params=pltpu.CompilerParams(

time: 87.7 us -> 93.6 us (1.067)
  Pallas kernels: 85.6 us -> 91.5 us
    pallas_call x1, Pallas kernels: 85.6 us -> 91.5 us  [kernel_shards(): pl.pallas_call(block_kernel, out_shape=jax.ShapeDtypeStruct((rows, width)...]
where the time goes in v2:
time: 93.6 us; the launch traced here: 93.4 us
  Pallas kernels  91.5 us (98%)
  local copies, waits for them, and re-layouts  1.89 us (2%)
    pallas_call x1, Pallas kernels, kernel_shards(): pl.pallas_call(block_kernel, out_shape=jax.ShapeDtypeStruct((rows, width)...  91.5 us
    unnamed x1, local copies, waits for them, and re-layouts  1.89 us

profile of v2, /device:TPU:16, one launch (start us, length us, event | category | flops | bytes accessed | tf_op | source)
XLA Modules:
  0.0 93.4 jit_solution(2518858342362330560)
XLA Ops:
  0.0 91.5 %shard_map.100 = f32[128,1024]{1,0:T(8,128)} custom-call(f32[128,1024]{1,0:T(8,128)} %x_hbm.1, f32[1,4096]{1,0:T(1,128)} %bitcast.1, bf16[3,1024,512]{2,1,0:T(8,128)(2,1)} %w_hbm.1, f32[3,3,512]{2,1,0:T(4,128)} %taps_hbm.1, f32[128,512]{1,0:T(8,128)} %filter_hbm.1, bf16[1024,512]{1,0:T(8,128)(2,1)} %wo_hbm.1, bf16[1024,512]{1,0:T(8,128)(2,1)} %constant.8.clone.ah_hbm, ...), custom_call_target="tpu_custom_call" | custom-call | tf_op jit(solution)/shard_map/pallas_call | solution.py:491
  91.5 1.9 %copy.12 = f32[128,1024]{1,0:T(8,128)} copy(f32[128,1024]{1,0:T(8,128)} %shard_map.100) | data formatting | bytes 1048576
